TPU v7x, 128 devices: a whole 4x4x4 slice. The times are simulated.
128 devices in a mesh: dp: 4 (over z), row: 4 (over x_lo, core), col: 8 (over x_hi, y).
Axes of the slice: x: 4 (x_hi: 2, x_lo: 2; x = x_hi * 2 + x_lo), y: 4, z: 4, core: 2. Of those that a mesh axis runs over, the one named last changes fastest.
Arguments:
- activations: bfloat16 [4096, 18432], P(('dp', 'col'), 'row'), may hold values from -6 to 6
- cotangent: bfloat16 [4096, 16384], P(('dp', 'row'), 'col'), may hold values from -0.09375 to 0.09375
- weight: float32 [18432, 16384], P(('row', 'dp'), 'col'), may hold values from -60 to 60
- row_moment: float32 [18432], P(('row', 'dp')), may hold values from 0.05 to 1
- col_moment: float32 [16384], P('col'), may hold values from 0.05 to 1
Outputs:
- new_weight: float32 [18432, 16384], P(('row', 'dp'), 'col')
- clipped_update: bfloat16 [18432, 16384], P(('row', 'dp'), 'col')
- new_row_moment: float32 [18432], P(('row', 'dp'))
- new_col_moment: float32 [16384], P('col')
All inputs are finite; a program needn't handle non-finite values.
Results may differ from a plain program's by a relative error of at most 0.001.
Values may be sent and summed in bfloat16 or wider, within the bound.
A program may use at most 192 MiB of HBM per device.

v0:
```python
import jax
import jax.numpy as jnp
from jax import lax
from jax.sharding import PartitionSpec as P

D = 18432
F = 16384
STEP = 10


def token_product(left, right):
    return lax.dot_general(
        left, right, (((0,), (0,)), ((), ())), preferred_element_type=jnp.float32
    )


def body(activations, cotangent, weight, row_moment, col_moment):
    decay_rate = 1.0 - float(STEP) ** (-0.8)
    relative = min(0.01, float(STEP) ** (-0.5))
    act_rows = lax.all_gather(activations, "col", axis=0, tiled=True)
    cot_rows = lax.all_gather(cotangent, "row", axis=0, tiled=True)
    gradient = lax.psum_scatter(
        token_product(act_rows, cot_rows), "dp", scatter_dimension=0, tiled=True
    )
    squared = gradient * gradient
    row_sum = lax.psum(jnp.sum(squared, axis=1), "col")
    col_sum = lax.psum(jnp.sum(squared, axis=0), ("dp", "row"))
    row_new = decay_rate * row_moment + (1.0 - decay_rate) * row_sum / F
    col_new = decay_rate * col_moment + (1.0 - decay_rate) * col_sum / D
    update = gradient * lax.rsqrt(row_new)[:, None] * lax.rsqrt(col_new)[None, :]
    update_total = lax.psum(jnp.sum(update * update), ("dp", "row", "col"))
    clip_factor = jnp.maximum(1.0, jnp.sqrt(update_total / (D * F)))
    clipped = update / clip_factor
    new_weight = weight - relative * clipped
    return (new_weight, clipped.astype(jnp.bfloat16), row_new, col_new)


def solution(mesh):
    placed = (
        P(("dp", "col"), "row"),
        P(("dp", "row"), "col"),
        P(("row", "dp"), "col"),
        P(("row", "dp")),
        P("col"),
    )
    return jax.shard_map(
        body,
        mesh=mesh,
        in_specs=placed,
        out_specs=(P(("row", "dp"), "col"), P(("row", "dp"), "col"), P(("row", "dp")), P("col")),
        check_vma=False,
    )
```

profile of v0, /device:TPU:1, one launch (start us, length us, event | category | flops | bytes accessed | tf_op | source)
XLA Modules:
  0.0 669.9 jit_solution(4556343344577796499)
XLA Ops:
  7.2 0.0 all-gather.5.cloned.1.call-start
  7.2 0.7 all-gather.5.cloned.1.call-update
  7.9 0.0 all-gather.3.cloned.1.call-start
  7.9 0.7 all-gather.3.cloned.1.call-update
  8.6 0.0 reduce-scatter.2.cloned.1.call-start
  8.7 51.1 %all-gather.5.cloned.1.call-done = bf16[1024,2048]{1,0:T(8,128)(2,1)} async-done(((bf16[256,2048]{1,0:T(8,128)(2,1)}), bf16[1024,2048]{1,0:T(8,128)(2,1)}) %all-gather.5.cloned.1.call-update) | async-done | bytes 4194320 | tf_op jit(solution)/shard_map/all_gather | solution.py:21
  59.8 118.8 %all-gather.3.cloned.1.call-done = bf16[1024,4608]{1,0:T(8,128)(2,1)} async-done(((bf16[128,4608]{1,0:T(8,128)(2,1)}), bf16[1024,4608]{1,0:T(8,128)(2,1)}) %all-gather.3.cloned.1.call-update) | async-done | bytes 9437200 | tf_op jit(solution)/shard_map/all_gather | solution.py:20
  178.7 28.0 %fusion.4 = f32[4608,2048]{1,0:T(8,128)} fusion(bf16[1024,4608]{1,0:T(8,128)(2,1)} %all-gather.3.cloned.1.call-done, bf16[1024,2048]{1,0:T(8,128)(2,1)} %all-gather.5.cloned.1.call-done), kind=kOutput, calls=%fused_computation.11 | convolution fusion | flops 19327352832 | bytes 51380224 | tf_op jit(solution)/shard_map/dot_general | solution.py:12
  206.7 0.0 reduce-scatter.2.cloned.1.call-update
  206.7 0.0 copy-start
  206.7 0.0 copy-start.1
  206.7 315.2 %reduce-scatter.2.cloned.1.call-done = f32[1152,2048]{1,0:T(8,128)} async-done(((f32[4608,2048]{1,0:T(8,128)}), f32[1152,2048]{1,0:T(8,128)}) %reduce-scatter.2.cloned.1.call-update) | async-done | bytes 9437200 | tf_op jit(solution)/shard_map/reduce_scatter | solution.py:22
  522.0 4.7 multiply_reduce_fusion.2
  526.7 20.6 %psum.21 = f32[1152]{0:T(1024)S(1)} all-reduce(f32[1152]{0:T(1024)S(1)} %get-tuple-element.4), channel_id=1, replica_groups=mesh['dp'=4,'row'=4,'col'=8] {'col'}, use_global_device_ids=true, to_apply=%region_2.0 | all-reduce | flops 1152 | bytes 9216 | tf_op jit(solution)/shard_map/psum | solution.py:26
  547.3 31.3 %psum.22 = f32[2048]{0:T(1024)S(1)} all-reduce(f32[2048]{0:T(1024)S(1)} %get-tuple-element.5), channel_id=1, replica_groups=mesh['dp'=4,'row'=4,'col'=8] {'dp','row'}, use_global_device_ids=true, to_apply=%region_4.0 | all-reduce | flops 2048 | bytes 16384 | tf_op jit(solution)/shard_map/psum | solution.py:27
  578.6 0.0 copy-done
  578.6 0.6 fusion.3
  579.2 0.0 copy-done.1
  579.2 0.6 fusion.2
  579.8 7.0 %multiply_reduce_fusion = f32[]{:T(128)} fusion(f32[1152,2048]{1,0:T(8,128)} %reduce-scatter.2.cloned.1.call-done, f32[2048]{0:T(1024)S(1)} %get-tuple-element.8, f32[1152]{0:T(1024)S(1)} %get-tuple-element.6), kind=kLoop, calls=%fused_computation.1 | loop fusion | flops 9437183 | bytes 9449988 | tf_op jit(solution)/shard_map/reduce_sum | solution.py:31
  586.9 62.2 %psum.23 = f32[]{:T(128)} all-reduce(f32[]{:T(128)} %multiply_reduce_fusion), channel_id=1, replica_groups=mesh['dp'=4,'row'=4,'col'=8] {'dp','row','col'}, use_global_device_ids=true, to_apply=%region_6.0 | all-reduce | flops 1 | bytes 8 | tf_op jit(solution)/shard_map/psum | solution.py:31
  649.7 13.6 %fusion.1 = (bf16[1152,2048]{1,0:T(8,128)(2,1)}, f32[1152,2048]{1,0:T(8,128)}) fusion(f32[]{:T(128)S(6)} %max_shard_map.3, f32[2048]{0:T(1024)S(1)} %get-tuple-element.8, f32[1152,2048]{1,0:T(8,128)} %reduce-scatter.2.cloned.1.call-done, f32[1152]{0:T(1024)S(1)} %get-tuple-element.6, f32[1152,2048]{1,0:T(8,128)} %param.7), kind=kLoop, calls=%fused_computation.6 | loop fusion | flops 14155776 | bytes 33042948 | tf_op jit(solution)/shard_map/convert_element_type | solution.py:35
Async XLA Ops:
  7.2 52.7 %all-gather.5.cloned.1.call-start = ((), (), s32[]{:S(2)}) async-start(), calls=%async_computation.2 | async-start | bytes 5242880 | tf_op jit(solution)/shard_map/all_gather | solution.py:21
  7.9 170.8 %all-gather.3.cloned.1.call-start = ((), (), s32[]{:S(2)}) async-start(), calls=%async_computation.1 | async-start | bytes 10616832 | tf_op jit(solution)/shard_map/all_gather | solution.py:20
  8.6 513.3 %reduce-scatter.2.cloned.1.call-start = ((), (), s32[]{:S(2)}) async-start(), calls=%async_computation.3 | async-start | bytes 47185920 | tf_op jit(solution)/shard_map/reduce_scatter | solution.py:22
  206.7 371.9 %copy-start = (f32[2048]{0:T(1024)S(1)}, f32[2048]{0:T(1024)}, u32[]{:S(2)}) copy-start(f32[2048]{0:T(1024)} %param.9) | copy-start | bytes 24580
  206.7 372.5 %copy-start.1 = (f32[1152]{0:T(1024)S(1)}, f32[1152]{0:T(1024)}, u32[]{:S(2)}) copy-start(f32[1152]{0:T(1024)} %param.8) | copy-start | bytes 13828
Sparse Core Ops, SparseCore 0:
  9.7 50.1 all-gather.4
  62.1 116.4 all-gather.2
  206.8 315.0 reduce-scatter.1
where the time goes:
time: 670 us
  waiting for transfers between devices  487 us (73%)
  blocking collectives  114 us (17%)
  matrix products  28 us (4%)
  other arithmetic  26.6 us (4%)
  between operations  14.5 us (2%)
    reduce_scatter x1, waiting for transfers between devices, body(): lax.psum_scatter(token_product(act_rows, cot_rows), 'dp', scatter_dimensi...  315 us
    all_gather x1, waiting for transfers between devices, body(): act_rows = lax.all_gather(activations, 'col', axis=0, tiled=True)  119 us
    psum x1, blocking collectives, body(): update_total = lax.psum(jnp.sum(update * update), ('dp', 'row', 'col'))  62.2 us
    all_gather x1, waiting for transfers between devices, body(): cot_rows = lax.all_gather(cotangent, 'row', axis=0, tiled=True)  51.1 us
    psum x1, blocking collectives, body(): col_sum = lax.psum(jnp.sum(squared, axis=0), ('dp', 'row'))  31.3 us
    dot_general x1, matrix products, token_product(): lax.dot_general(left, right, (((0,), (0,)), ((), ())), preferred_element_...  28 us
    psum x1, blocking collectives, body(): row_sum = lax.psum(jnp.sum(squared, axis=1), 'col')  20.6 us
    convert_element_type x1, other arithmetic, body(): return (new_weight, clipped.astype(jnp.bfloat16), row_new, col_new)  13.6 us
  transfers between devices with their start and end apart: 3, of which 3 were waited for; matrix products, arithmetic and copies ran while one was open for 0% of the time, Pallas kernels for 0%

commit v1 on v0

v1 whole, which is shorter than its diff:
```python
import functools

import jax
import jax.numpy as jnp
from jax import lax
from jax.experimental import pallas as pl
from jax.experimental.pallas import tpu as pltpu
from jax.sharding import PartitionSpec as P

D = 18432
F = 16384
STEP = 10
MESH = pl.DeviceIdType.MESH

ROWS = 1152
COLS = 2048
PIECE = 128
PIECES = 32
TILE = 512
SENDS = 62


def gather_kernel(
    act, cot, weight, row_m, col_m,
    u_ref, w_ref, scale_ref, row_out, col_out,
    a_in, a_src, at, ct, row_part, row_col, col_scale, row_x, col_x, tot_a, tot_b,
    load_sem, send_sem, a_sem, c_sem, own_sem, x_send, y_send, row_sem, col_sem, ta_sem, tb_sem,
):
    z, row, col = lax.axis_index("dp"), lax.axis_index("row"), lax.axis_index("col")
    x_lo, core = row // 2, row % 2
    x_hi, y = col // 4, col % 4
    group = z * 4 + row

    def a_id(zo, xo, yo):
        return ((z + zo + 4) % 4) * 8 + ((x_hi + xo) % 2) * 4 + (y + yo + 4) % 4

    def c_id(zo, xo, co, half):
        return ((z + zo + 4) % 4) * 8 + ((x_lo + xo) % 2) * 4 + ((core + co) % 2) * 2 + half

    def at_z(o):
        return {"dp": (z + o + 4) % 4, "row": row, "col": col}

    def at_y(o):
        return {"dp": z, "row": row, "col": x_hi * 4 + (y + o + 4) % 4}

    def at_x_hi():
        return {"dp": z, "row": row, "col": (1 - x_hi) * 4 + y}

    def at_x_lo():
        return {"dp": z, "row": (1 - x_lo) * 2 + core, "col": col}

    def at_core():
        return {"dp": z, "row": x_lo * 2 + 1 - core, "col": col}

    def col_peer(i):
        return {"dp": z, "row": row, "col": (col + i) % 8}

    def group_peer(i):
        g = (group + i) % 16
        return {"dp": g // 4, "row": g % 4, "col": col}

    barrier = pltpu.get_barrier_semaphore()

    def greet_col(i, carry):
        pl.semaphore_signal(barrier, inc=1, device_id=col_peer(i), device_id_type=MESH)
        return carry

    def greet_group(i, carry):
        pl.semaphore_signal(barrier, inc=1, device_id=group_peer(i), device_id_type=MESH)
        return carry

    load_act = pltpu.make_async_copy(act, a_in, load_sem.at[0])
    load_act.start()
    load_cot = []
    for half in range(2):
        load_cot.append(pltpu.make_async_copy(
            cot.at[pl.ds(half * PIECE, PIECE)], ct.at[c_id(0, 0, 0, half)], load_sem.at[1 + half]
        ))
        load_cot[half].start()
    lax.fori_loop(1, 8, greet_col, 0)
    lax.fori_loop(1, 16, greet_group, 0)

    sent = []

    def push(src, dst, sem, device):
        copy = pltpu.make_async_remote_copy(
            src_ref=src, dst_ref=dst, send_sem=send_sem.at[len(sent)], recv_sem=sem,
            device_id=device, device_id_type=MESH,
        )
        copy.start()
        sent.append(copy)

    def push_a(t, device):
        push(at.at[t], at.at[t], a_sem.at[t], device)

    def push_c(t, device):
        push(ct.at[t], ct.at[t], c_sem.at[t], device)

    def wait_a(zo, xo, yo):
        t = a_id(zo, xo, yo)
        pltpu.make_async_copy(at.at[t], at.at[t], a_sem.at[t]).wait()
        return t

    def wait_c(zo, xo, co, half):
        t = c_id(zo, xo, co, half)
        pltpu.make_async_copy(ct.at[t], ct.at[t], c_sem.at[t]).wait()
        return t

    def turned(slot, block):
        start = pl.multiple_of(slot * ROWS + block * 128, 128)
        return a_in[:, pl.ds(start, 128)].T

    def ring(t, *steps):
        for o in steps:
            push_a(t, at_y(o))

    load_act.wait()
    own = a_id(0, 0, 0)
    for block in range(ROWS // 128):
        at[own, pl.ds(block * 128, 128), :] = turned(z, block)
    pl.semaphore_wait(barrier, 22)
    ring(own, 1, -1)
    push_a(own, at_x_hi())
    for i, o in enumerate((1, -1, 2)):
        for block in range(ROWS // 128):
            a_src[i, pl.ds(block * 128, 128), :] = turned((z + o + 4) % 4, block)
        push(a_src.at[i], at.at[own], a_sem.at[own], at_z(o))
    for half in range(2):
        load_cot[half].wait()
    mine = [c_id(0, 0, 0, half) for half in range(2)]
    for half in range(2):
        push_c(mine[half], at_z(1))
        push_c(mine[1 - half], at_z(-1))
        push_c(mine[half], at_core())
    load_weight = pltpu.make_async_copy(weight, w_ref, load_sem.at[3])
    load_weight.start()

    def matmul(ids, first=False, last=False):
        def tile(j, carry):
            s = pl.ds(pl.multiple_of(j * TILE, TILE), TILE)
            left = jnp.concatenate([at[t] for t in ids], axis=1)
            right = jnp.concatenate([ct[t, :, s] for t in ids], axis=0)
            product = jnp.dot(left, right, preferred_element_type=jnp.float32)
            if not first:
                product = u_ref[:, s] + product
            u_ref[:, s] = product
            if last:
                square = product * product
                col_x[group, :, s] = jnp.sum(square, axis=0, keepdims=True)
                part = square[:, :128]
                for k in range(1, TILE // 128):
                    part = part + square[:, k * 128:(k + 1) * 128]
                row_part[...] += part
            return carry

        lax.fori_loop(0, COLS // TILE, tile, 0)

    def cot_group(zo, xo):
        return [c_id(zo, xo, co, half) for co in range(2) for half in range(2)]

    t = wait_a(0, 1, 0)
    ring(t, 1, -1)
    t = wait_a(1, 0, 0)
    ring(t, 1, -1)
    push_a(t, at_x_hi())
    t = wait_a(-1, 0, 0)
    push_a(t, at_x_hi())
    t = wait_a(2, 0, 0)
    push_a(t, at_x_hi())
    for half in range(2):
        push_c(mine[half], at_x_lo())
    ring(wait_a(0, 0, -1), 1)
    wait_a(0, 0, 1)
    ring(wait_a(0, 1, 1), -1)
    wait_a(0, 1, -1)
    ring(wait_a(1, 1, 0), 1, -1)
    ring(wait_a(1, 0, -1), 1)
    wait_a(1, 0, 1)
    ring(a_id(-1, 0, 0), 1, -1)
    third = wait_a(-1, 1, 0)
    ring(third, 1)
    for half in range(2):
        t = wait_c(-1, 0, 0, 0) if half == 0 else wait_c(1, 0, 0, 1)
        push_c(t, at_z(1 - 2 * half))
        push_c(t, at_core())
    wait_a(0, 0, 2)
    wait_a(0, 1, 2)
    for half in range(2):
        wait_c(0, 0, 1, half)
    row_x[col] = jnp.zeros((16, 128), jnp.float32)
    row_part[...] = jnp.zeros_like(row_part)
    matmul(cot_group(0, 0), first=True)
    ring(wait_a(1, 1, 1), -1)
    ring(third, -1)
    wait_a(1, 1, -1)
    push_c(wait_c(-1, 0, 0, 1), at_core())
    push_c(wait_c(1, 0, 0, 0), at_core())
    t = wait_c(0, 1, 0, 0)
    for device in (at_z(1), at_z(-1), at_core()):
        push_c(t, device)
    wait_a(-1, 0, 1)
    ring(wait_a(-1, 0, -1), 1)
    ring(a_id(2, 0, 0), 1)
    last = wait_a(2, 1, 0)
    ring(last, 1, -1)
    wait_a(1, 0, 2)
    wait_a(1, 1, 2)
    for zo in (1, -1):
        for half in range(2):
            wait_c(zo, 0, 1, half)
    matmul(cot_group(1, 0))
    for half in range(2):
        t = wait_c(2, 0, 0, half)
        push_c(t, at_x_lo())
        push_c(t, at_core())
    t = wait_c(0, 1, 0, 1)
    for device in (at_z(1), at_z(-1), at_core()):
        push_c(t, device)
    ring(wait_a(-1, 1, 1), -1)
    ring(a_id(2, 0, 0), -1)
    wait_a(-1, 1, -1)
    for half in range(2):
        wait_c(0, 1, 1, half)
    matmul(cot_group(0, 1))
    ring(wait_a(2, 1, 1), -1)
    for zo in (-1, 1):
        push_c(wait_c(zo, 1, 0, 0), at_core())
    ring(wait_a(2, 0, -1), 1)
    wait_a(-1, 0, 2)
    wait_a(-1, 1, 2)
    matmul(cot_group(-1, 0))
    push_c(wait_c(2, 1, 0, 0), at_core())
    for zo in (-1, 1):
        wait_c(zo, 1, 1, 0)
    matmul([c_id(zo, 1, co, 0) for zo in (-1, 1) for co in range(2)])
    for zo in (-1, 1):
        push_c(wait_c(zo, 1, 0, 1), at_core())
    push_c(wait_c(2, 1, 0, 1), at_core())
    for zo in (-1, 1):
        wait_c(zo, 1, 1, 1)
    matmul([c_id(zo, 1, co, 1) for zo in (-1, 1) for co in range(2)])
    for xo in range(2):
        for half in range(2):
            wait_c(2, xo, 1, half)
    wait_a(2, 0, 1)
    wait_a(2, 1, -1)
    matmul([a_id(2, xo, yo) for xo in range(2) for yo in (0, 1)])
    matmul([a_id(2, xo, -1) for xo in range(2)])
    wait_a(2, 0, 2)
    wait_a(2, 1, 2)
    matmul([a_id(2, xo, 2) for xo in range(2)], last=True)

    def small(buf, slot, sem, sends, peer, count):
        def descriptor(i):
            return pltpu.make_async_remote_copy(
                src_ref=buf.at[slot], dst_ref=buf.at[slot], send_sem=sends.at[i], recv_sem=sem.at[slot],
                device_id=peer(i), device_id_type=MESH,
            )

        def start(i, carry):
            descriptor(i).start()
            return carry

        def finish(i, carry):
            other = (slot + i) % count
            pltpu.make_async_copy(buf.at[other], buf.at[other], sem.at[other]).wait()
            return carry

        def drain(i, carry):
            descriptor(i).wait_send()
            return carry

        return (
            lambda: lax.fori_loop(1, count, start, 0),
            lambda: lax.fori_loop(1, count, finish, 0),
            lambda: lax.fori_loop(1, count, drain, 0),
        )

    col_start, col_finish, col_drain = small(col_x, group, col_sem, x_send, group_peer, 16)
    row_start, row_finish, row_drain = small(row_x, col, row_sem, y_send, col_peer, 8)
    col_start()
    for block in range(ROWS // 128):
        turned_part = row_part[pl.ds(block * 128, 128), :].T
        row_x[col, pl.ds(block, 1), :] = jnp.sum(turned_part, axis=0, keepdims=True)
    row_start()
    for copy in sent:
        copy.wait_send()
    load_weight.wait()

    decay_rate = 1.0 - float(STEP) ** (-0.8)
    col_finish()
    col_sum = col_x[0]
    for i in range(1, 16):
        col_sum = col_sum + col_x[i]
    col_new = decay_rate * col_m[...] + (1.0 - decay_rate) * col_sum / D
    col_out[...] = col_new
    col_scale[...] = lax.rsqrt(col_new)
    row_finish()
    row_sum = row_x[0]
    for i in range(1, 8):
        row_sum = row_sum + row_x[i]
    row_new = decay_rate * row_m[...] + (1.0 - decay_rate) * row_sum[: ROWS // 128] / F
    row_out[...] = row_new
    row_scale = lax.rsqrt(row_new)
    for block in range(ROWS // 128):
        spread = jnp.broadcast_to(row_scale[block:block + 1, :], (128, 128))
        row_col[pl.ds(block * 128, 128), :] = spread.T

    def scale_rows(block, total):
        r = pl.ds(pl.multiple_of(block * 64, 64), 64)
        factor = row_col[r, :]
        for k in range(COLS // 128):
            s = pl.ds(k * 128, 128)
            update = u_ref[r, s] * factor * col_scale[:, s]
            u_ref[r, s] = update
            total = total + update * update
        return total

    total = lax.fori_loop(0, ROWS // 64, scale_rows, jnp.zeros((64, 128), jnp.float32))
    tot_a[group] = jnp.sum(total.reshape(8, 8, 128), axis=0)
    col_drain()
    row_drain()
    a_start, a_finish, a_drain = small(tot_a, group, ta_sem, x_send, group_peer, 16)
    a_start()
    a_finish()
    total = tot_a[0]
    for i in range(1, 16):
        total = total + tot_a[i]
    tot_b[col] = total
    b_start, b_finish, b_drain = small(tot_b, col, tb_sem, y_send, col_peer, 8)
    b_start()
    a_drain()
    b_finish()
    total = tot_b[0]
    for i in range(1, 8):
        total = total + tot_b[i]
    mean = jnp.sum(total, keepdims=True) / (D * F)
    clip_factor = jnp.maximum(1.0, jnp.sqrt(mean))
    scale_ref[...] = jnp.broadcast_to(1.0 / clip_factor, (8, 128))
    b_drain()


def write_kernel(u_ref, w_ref, scale_ref, new_weight, clipped, stage_w, stage_c, sem):
    relative = min(0.01, float(STEP) ** (-0.5))
    height, slots = 128, 3
    steps = ROWS // height

    def copies(i):
        r = pl.ds(i * height, height)
        s = i % slots
        return (
            pltpu.make_async_copy(stage_w.at[s], new_weight.at[r], sem.at[s, 0]),
            pltpu.make_async_copy(stage_c.at[s], clipped.at[r], sem.at[s, 1]),
        )

    scale = scale_ref[0:1, :]
    for i in range(steps):
        if i >= slots:
            for copy in copies(i - slots):
                copy.wait()
        r = pl.ds(i * height, height)
        for k in range(COLS // 128):
            s = pl.ds(k * 128, 128)
            value = u_ref[r, s] * scale
            stage_c[i % slots, :, s] = value.astype(jnp.bfloat16)
            stage_w[i % slots, :, s] = w_ref[r, s] - relative * value
        for copy in copies(i):
            copy.start()
    for i in range(steps - slots, steps):
        for copy in copies(i):
            copy.wait()


def body(activations, cotangent, weight, row_moment, col_moment):
    f32, bf16 = jnp.float32, jnp.bfloat16
    vmem, anywhere = pl.BlockSpec(memory_space=pltpu.VMEM), pl.BlockSpec(memory_space=pl.ANY)
    update, held, scale, row_new, col_new = pl.pallas_call(
        gather_kernel,
        out_shape=(
            pltpu.VMEM((ROWS, COLS), f32),
            pltpu.VMEM((ROWS, COLS), f32),
            jax.ShapeDtypeStruct((8, 128), f32),
            jax.ShapeDtypeStruct((ROWS // 128, 128), f32),
            jax.ShapeDtypeStruct((1, COLS), f32),
        ),
        in_specs=[anywhere, anywhere, anywhere, vmem, vmem],
        out_specs=(vmem,) * 5,
        scratch_shapes=[
            pltpu.VMEM((PIECE, 4 * ROWS), bf16),
            pltpu.VMEM((3, ROWS, PIECE), bf16),
            pltpu.VMEM((PIECES, ROWS, PIECE), bf16),
            pltpu.VMEM((PIECES, PIECE, COLS), bf16),
            pltpu.VMEM((ROWS, 128), f32),
            pltpu.VMEM((ROWS, 128), f32),
            pltpu.VMEM((1, COLS), f32),
            pltpu.VMEM((8, 16, 128), f32),
            pltpu.VMEM((16, 1, COLS), f32),
            pltpu.VMEM((16, 8, 128), f32),
            pltpu.VMEM((8, 8, 128), f32),
            pltpu.SemaphoreType.DMA((4,)),
            pltpu.SemaphoreType.DMA((SENDS,)),
            pltpu.SemaphoreType.DMA((PIECES,)),
            pltpu.SemaphoreType.DMA((PIECES,)),
            pltpu.SemaphoreType.DMA((1,)),
            pltpu.SemaphoreType.DMA((16,)),
            pltpu.SemaphoreType.DMA((8,)),
            pltpu.SemaphoreType.DMA((8,)),
            pltpu.SemaphoreType.DMA((16,)),
            pltpu.SemaphoreType.DMA((16,)),
            pltpu.SemaphoreType.DMA((8,)),
        ],
        compiler_params=pltpu.CompilerParams(
            collective_id=0, has_side_effects=True, vmem_limit_bytes=36 << 20
        ),
    )(activations, cotangent, weight, row_moment.reshape(ROWS // 128, 128), col_moment.reshape(1, COLS))
    new_weight, clipped = pl.pallas_call(
        write_kernel,
        out_shape=(
            jax.ShapeDtypeStruct((ROWS, COLS), f32),
            jax.ShapeDtypeStruct((ROWS, COLS), bf16),
        ),
        in_specs=[vmem, vmem, vmem],
        out_specs=(anywhere, anywhere),
        scratch_shapes=[
            pltpu.VMEM((3, 128, COLS), f32),
            pltpu.VMEM((3, 128, COLS), bf16),
            pltpu.SemaphoreType.DMA((3, 2)),
        ],
        compiler_params=pltpu.CompilerParams(vmem_limit_bytes=16 << 20),
    )(update, held, scale)
    return new_weight, clipped, row_new.reshape(ROWS), col_new.reshape(COLS)


def solution(mesh):
    placed = (
        P(("dp", "col"), "row"),
        P(("dp", "row"), "col"),
        P(("row", "dp"), "col"),
        P(("row", "dp")),
        P("col"),
    )
    return jax.shard_map(
        body,
        mesh=mesh,
        in_specs=placed,
        out_specs=(P(("row", "dp"), "col"), P(("row", "dp"), "col"), P(("row", "dp")), P("col")),
        check_vma=False,
    )
```

time: 670 us -> 122 us (0.18)
  waiting for transfers between devices: 487 us -> 0 us
  Pallas kernels: 0 us -> 119 us
  blocking collectives: 114 us -> 0 us
  matrix products: 28 us -> 0 us
  other arithmetic: 26.6 us -> 0 us
  between operations: 14.5 us -> 0.67 us
    reduce_scatter x1 -> x0, waiting for transfers between devices: 315 us -> none  [body(): lax.psum_scatter(token_product(act_rows, cot_rows), 'dp', scatter_dimensi...]
    all_gather x2 -> x0, waiting for transfers between devices: 170 us -> none  [the longest x1 119 us: body(): act_rows = lax.all_gather(activations, 'col', axis=0, tiled=True)]
    pallas_call x0 -> x2, Pallas kernels: none -> 119 us  [the longest x1 113 us: body(): pl.pallas_call(gather_kernel, out_shape=(pltpu.VMEM((ROWS, COLS), f32), p...]
    psum x3 -> x0, blocking collectives: 114 us -> none  [the longest x1 62.2 us: body(): update_total = lax.psum(jnp.sum(update * update), ('dp', 'row', 'col'))]
    dot_general x1 -> x0, matrix products: 28 us -> none  [token_product(): lax.dot_general(left, right, (((0,), (0,)), ((), ())), preferred_element_...]
    convert_element_type x1 -> x0, other arithmetic: 13.6 us -> none  [body(): return (new_weight, clipped.astype(jnp.bfloat16), row_new, col_new)]
    reduce_sum x2 -> x0, other arithmetic: 11.7 us -> none  [the longest x1 7.04 us: body(): update_total = lax.psum(jnp.sum(update * update), ('dp', 'row', 'col'))]
  transfers between devices with their start and end apart: 3 -> 0, of which waited for: 3 -> 0; matrix products, arithmetic and copies ran while one was open for 0% -> 0% of each run, Pallas kernels for 0% -> 0%
where the time goes in v1:
time: 122 us; the launch traced here: 121 us
  Pallas kernels  119 us (98%)
  local copies, waits for them, and re-layouts  1.88 us (2%)
    pallas_call x1, Pallas kernels, body(): pl.pallas_call(gather_kernel, out_shape=(pltpu.VMEM((ROWS, COLS), f32), p...  113 us
    pallas_call x1, Pallas kernels, body(): pl.pallas_call(write_kernel, out_shape=(jax.ShapeDtypeStruct((ROWS, COLS)...  5.32 us

profile of v1, /device:TPU:1, one launch (start us, length us, event | category | flops | bytes accessed | tf_op | source)
XLA Modules:
  0.0 121.3 jit_solution(9406021803543680357)
XLA Ops:
  0.6 113.4 %shard_map.84 = (f32[1152,2048]{1,0:T(8,128)S(1)}, f32[1152,2048]{1,0:T(8,128)S(1)}, f32[8,128]{1,0:T(8,128)}, f32[9,128]{1,0:T(8,128)}, f32[1,2048]{1,0:T(1,128)}) custom-call(bf16[128,4608]{1,0:T(8,128)(2,1)} %act.1, bf16[256,2048]{1,0:T(8,128)(2,1)} %cot.1, f32[1152,2048]{1,0:T(8,128)} %weight.1, f32[9,128]{1,0:T(8,128)} %bitcast.6, f32[1,2048]{1,0:T(1,128)} %bitcast.7), custom_call_target="tpu_custom_call" | custom-call | tf_op jit(solution)/shard_map/pallas_call | solution.py:377
  114.1 0.0 copy-start
  114.1 0.7 copy-done
  114.8 0.0 copy-start.2
  114.8 0.0 copy-start.1
  114.8 5.3 %shard_map.85 = (f32[1152,2048]{1,0:T(8,128)}, bf16[1152,2048]{1,0:T(8,128)(2,1)}) custom-call(f32[1152,2048]{1,0:T(8,128)S(1)} %get-tuple-element.11.u_ref, f32[1152,2048]{1,0:T(8,128)S(1)} %get-tuple-element.12.w_ref, f32[8,128]{1,0:T(8,128)S(1)} %copy-done), custom_call_target="tpu_custom_call" | custom-call | tf_op jit(solution)/shard_map/pallas_call | solution.py:416
  120.1 0.0 copy-done.2
  120.1 0.6 copy.11
  120.7 0.0 copy-done.1
  120.7 0.6 copy.12
Async XLA Ops:
  114.1 0.7 copy-start
  114.8 5.3 %copy-start.2 = (f32[9,128]{1,0:T(8,128)S(1)}, f32[9,128]{1,0:T(8,128)}, u32[]{:S(2)}) copy-start(f32[9,128]{1,0:T(8,128)} %get-tuple-element.16) | copy-start | bytes 13828
  114.8 5.9 %copy-start.1 = (f32[1,2048]{1,0:T(1,128)S(1)}, f32[1,2048]{1,0:T(1,128)}, u32[]{:S(2)}) copy-start(f32[1,2048]{1,0:T(1,128)} %get-tuple-element.17) | copy-start | bytes 24580

commit v2 on v0

v2 whole, which is shorter than its diff:
```python
import functools

import jax
import jax.numpy as jnp
from jax import lax
from jax.experimental import pallas as pl
from jax.experimental.pallas import tpu as pltpu
from jax.sharding import PartitionSpec as P

D = 18432
F = 16384
STEP = 10
MESH = pl.DeviceIdType.MESH

ROWS = 1152
COLS = 2048
PIECE = 128
PIECES = 32
SENDS = 66


PARTS = {
    "a0": (0, ROWS // 2), "a1": (ROWS // 2, ROWS // 2),
    "c0": (0, 32), "c1": (32, 32), "c2": (64, 64),
}
PART_SEM = {"a0": 0, "a1": 1, "c0": 0, "c1": 1, "c2": 2}
ORDER = (
    ("c>", (0, 0, 0, 0), "z+"), ("a>", (0, 0, 0), "z-"), ("c>", (0, 0, 0, 0), "core"), ("c>", (0, 0, 0, 1), "core"),
    ("c>", (0, 0, 0, 1), "z-"), ("c>", (0, 0, 0, 0), "x"), ("c<", (0, 0, 1, 0)), ("c<", (0, 0, 1, 1)),
    ("a>", (0, 0, 0), "z+"), ("a<", (0, 0, -1)), ("a>", (0, 0, -1), "y+"), ("a<", (0, 0, 1)), ("a<", (1, 0, 0)),
    ("a>", (1, 0, 0), "y-"), ("a<", (0, 1, 0)), ("a>", (0, 1, 0), "y+"), ("a>", (0, 1, 0), "y-"),
    ("c<", (-1, 0, 0, 0)), ("c>", (-1, 0, 0, 0), "core"), ("c>", (-1, 0, 0, 0), "z+"), ("c>", (0, 0, 0, 0), "z-"),
    ("a>", (1, 0, 0), "xh"), ("c<", (-1, 0, 1, 0)), ("a<", (0, 0, 2)), ("a>", (1, 0, 0), "y+"), ("a<", (1, 0, 1)),
    ("a>", (1, 0, 1), "y-"), ("a<", (-1, 0, 0)), ("c<", (1, 0, 0, 1)), ("c>", (1, 0, 0, 1), "core"),
    ("a>", (-1, 0, 0), "xh"), ("c<", (0, 1, 0, 0)), ("c>", (0, 1, 0, 0), "core"), ("c<", (1, 0, 1, 1)),
    ("a<", (0, 1, -1)), ("a>", (-1, 0, 0), "y+"), ("a<", (0, 1, 1)), ("a>", (0, 1, 1), "y-"), ("c<", (0, 1, 1, 0)),
    ("a>", (0, 0, 0), "z2"), ("a<", (1, 1, 0)), ("c>", (0, 0, 0, 1), "x"), ("a<", (1, 0, -1)),
    ("a>", (1, 1, 0), "y+"), ("a<", (1, 0, 2)), ("a>", (1, 1, 0), "y-"), ("c<", (2, 0, 0, 0)),
    ("c>", (2, 0, 0, 0), "core"), ("c>", (0, 0, 0, 1), "z+"), ("c>", (1, 0, 0, 1), "z-"), ("c<", (1, 0, 0, 0)),
    ("c>", (1, 0, 0, 0), "core"), ("a<", (-1, 1, 0)), ("c<", (2, 0, 1, 0)), ("c<", (1, 0, 1, 0)), ("a<", (-1, 0, -1)),
    ("a>", (-1, 1, 0), "y+"), ("a<", (0, 1, 2)), ("a>", (-1, 0, 0), "y-"), ("mm", "zero_near"),
    ("c2>", (2, 0, 0, 0), "x"), ("a<", (2, 0, 0)), ("a<", (1, 1, -1)), ("a>", (2, 0, 0), "y+"), ("a<", (1, 1, 1)),
    ("a>", (2, 0, 0), "y-"), ("c>", (0, 1, 0, 0), "z+"), ("c>", (0, 1, 0, 0), "z-"), ("a>", (2, 0, 0), "xh"),
    ("c<", (0, 1, 0, 1)), ("c>", (0, 1, 0, 1), "core"), ("c<", (0, 1, 1, 1)), ("mm", "zero_far"),
    ("a0>", (-1, 0, -1), "y+"), ("a>", (-1, 1, 0), "y-"), ("a<", (-1, 1, -1)), ("a<", (-1, 0, 1)),
    ("c<", (-1, 0, 0, 1)), ("c>", (-1, 0, 0, 1), "core"), ("c<", (2, 0, 0, 1)), ("c>", (2, 0, 0, 1), "core"),
    ("a>", (1, 0, 2), "xh"), ("c2<", (2, 1, 0, 0)), ("a>", (-1, 1, -1), "y+"), ("c<", (-1, 0, 1, 1)),
    ("c<", (2, 0, 1, 1)), ("c>", (0, 1, 0, 1), "z+"), ("c>", (0, 1, 0, 1), "z-"), ("a<", (2, 0, -1)),
    ("a<", (2, 0, 1)), ("a1>", (-1, 0, 1), "y-"), ("a<", (2, 1, 0)), ("c>", (2, 0, 0, 1), "x"), ("a0<", (-1, 0, 2)),
    ("a>", (2, 1, 0), "y+"), ("a>", (2, 1, 0), "y-"), ("c<", (-1, 1, 0, 0)), ("c>", (-1, 1, 0, 0), "core"),
    ("c<", (1, 1, 0, 0)), ("c>", (1, 1, 0, 0), "core"), ("a<", (-1, 1, 1)), ("a<", (1, 1, 2)), ("mm", "plus_near"),
    ("a>", (2, 0, -1), "y+"), ("c0>", (-1, 1, 0, 0), "z+"), ("c1>", (1, 1, 0, 0), "z-"), ("c<", (-1, 1, 1, 0)),
    ("c<", (1, 1, 1, 0)), ("a<", (-1, 1, 2)), ("a1<", (-1, 0, 2)), ("mm", "minus_near"), ("mm", "far_0"),
    ("a<", (2, 1, -1)), ("a<", (2, 1, 1)), ("a>", (2, 1, 1), "y-"), ("c<", (-1, 1, 0, 1)),
    ("c>", (-1, 1, 0, 1), "core"), ("c<", (1, 1, 0, 1)), ("c>", (1, 1, 0, 1), "core"), ("mm", "two_near"),
    ("c<", (2, 1, 0, 1)), ("c>", (2, 1, 0, 1), "core"), ("c<", (-1, 1, 1, 1)), ("c0<", (2, 1, 0, 0)),
    ("c1<", (2, 1, 0, 0)), ("c>", (2, 1, 0, 0), "core"), ("c<", (1, 1, 1, 1)), ("mm", "far_1"), ("c<", (2, 1, 1, 1)),
    ("a<", (2, 0, 2)), ("c<", (2, 1, 1, 0)), ("mm", "two_far"), ("a<", (2, 1, 2)), ("mm", "two_last"),
)


def gather_kernel(
    act, cot, weight, row_m, col_m,
    g_ref, w_ref, row_col, col_scale, row_out, col_out,
    a_in, a_src, at, ct, row_part, row_x, col_x, tot_a, tot_b,
    load_sem, send_sem, a_sem, c_sem, x_send, y_send, ta_send, tb_send, row_sem, col_sem, ta_sem, tb_sem,
):
    z, row, col = lax.axis_index("dp"), lax.axis_index("row"), lax.axis_index("col")
    x_lo, core = row // 2, row % 2
    x_hi, y = col // 4, col % 4
    group = z * 4 + row
    z_at = {o: lax.rem(z + o + 4, 4) for o in (0, 1, -1, 2)}
    y_at = {o: lax.rem(y + o + 4, 4) for o in (0, 1, -1, 2)}
    x_hi_at, x_lo_at, core_at = (x_hi, 1 - x_hi), (x_lo, 1 - x_lo), (core, 1 - core)

    def a_id(zo, xo, yo):
        return z_at[zo] * 8 + x_hi_at[xo] * 4 + y_at[yo]

    def c_id(zo, xo, co, half):
        return z_at[zo] * 8 + x_lo_at[xo] * 4 + core_at[co] * 2 + half

    place = {
        "z+": {"dp": z_at[1], "row": row, "col": col},
        "z-": {"dp": z_at[-1], "row": row, "col": col},
        "z2": {"dp": z_at[2], "row": row, "col": col},
        "y+": {"dp": z, "row": row, "col": x_hi * 4 + y_at[1]},
        "y-": {"dp": z, "row": row, "col": x_hi * 4 + y_at[-1]},
        "xh": {"dp": z, "row": row, "col": (1 - x_hi) * 4 + y},
        "x": {"dp": z, "row": (1 - x_lo) * 2 + core, "col": col},
        "core": {"dp": z, "row": x_lo * 2 + 1 - core, "col": col},
    }

    def col_peer(i):
        return {"dp": z, "row": row, "col": lax.rem(col + i, 8)}

    def group_peer(i):
        return {"dp": lax.rem(z + i // 4, 4), "row": lax.rem(row + i, 4), "col": col}

    def group_slot(i):
        return lax.rem(z + i // 4, 4) * 4 + lax.rem(row + i, 4)

    def col_slot(i):
        return lax.rem(col + i, 8)

    offsets = (0, 1, -1, 2)
    load_act = []
    for i, o in enumerate(offsets):
        start = pl.multiple_of(z_at[o] * ROWS, 128)
        load_act.append(pltpu.make_async_copy(act.at[:, pl.ds(start, ROWS)], a_in.at[i], load_sem.at[i]))
        load_act[i].start()
    mine = [c_id(0, 0, 0, half) for half in range(2)]
    load_cot = []
    for half in range(2):
        load_cot.append(pltpu.make_async_copy(
            cot.at[pl.ds(half * PIECE, PIECE)], ct.at[mine[half]], load_sem.at[4 + half]
        ))
        load_cot[half].start()

    barrier = pltpu.get_barrier_semaphore()
    for where in place.values():
        pl.semaphore_signal(barrier, inc=1, device_id=where, device_id_type=MESH)

    sent = []

    def push(src, dst, sem, device):
        copy = pltpu.make_async_remote_copy(
            src_ref=src, dst_ref=dst, send_sem=send_sem.at[len(sent)], recv_sem=sem,
            device_id=device, device_id_type=MESH,
        )
        copy.start()
        sent.append(copy)

    def piece(kind, key):
        if kind[0] == "a":
            t, whole, sem = a_id(*key), at, a_sem
        else:
            t, whole, sem = c_id(*key), ct, c_sem
        if kind in PARTS:
            return whole.at[t, pl.ds(*PARTS[kind])], sem.at[PIECES + PART_SEM[kind]]
        return whole.at[t], sem.at[t]

    def send(kind, key, where):
        ref, sem = piece(kind, key)
        push(ref, ref, sem, place[where])

    own = a_id(0, 0, 0)

    def turn(i, out):
        load_act[i].wait()
        for block in range(ROWS // 128):
            r = pl.ds(block * 128, 128)
            out[r, :] = a_in[i, :, r].T

    turn(0, at.at[own])
    pl.semaphore_wait(barrier, 8)
    for where in ("y+", "y-", "xh"):
        send("a", (0, 0, 0), where)
    for half in range(2):
        load_cot[half].wait()
    load_weight = pltpu.make_async_copy(weight, w_ref, load_sem.at[6])

    def matmul(ids, first=False, last=False, width=1024):
        def tile(j, carry):
            s = pl.ds(pl.multiple_of(j * width, width), width)
            left = jnp.concatenate([at[t] for t in ids], axis=1)
            right = jnp.concatenate([ct[t, :, s] for t in ids], axis=0)
            product = jnp.dot(left, right, preferred_element_type=jnp.float32)
            if not first:
                product = g_ref[:, s] + product
            g_ref[:, s] = product
            if last:
                square = product * product
                col_x[group, :, s] = jnp.sum(square, axis=0, keepdims=True)
                part = square[:, :128]
                for k in range(1, width // 128):
                    part = part + square[:, k * 128:(k + 1) * 128]
                row_part[...] += part
            return carry

        lax.fori_loop(0, COLS // width, tile, 0)

    def cot_group(zo, xo):
        return [c_id(zo, xo, co, half) for co in range(2) for half in range(2)]

    def far(half):
        return [c_id(zo, 1, co, half) for zo in (-1, 1) for co in range(2)]

    def early(half):
        return [z_at[2] * 8 + half * 4 + y_at[yo] for yo in (0, 1, -1)]

    groups = {
        "zero_near": cot_group(0, 0),
        "zero_far": cot_group(0, 1),
        "plus_near": cot_group(1, 0),
        "minus_near": cot_group(-1, 0),
        "far_0": far(0),
        "far_1": far(1),
        "two_near": early(x_lo),
        "two_far": early(1 - x_lo),
        "two_last": [a_id(2, xo, 2) for xo in range(2)],
    }

    multiplied = 0
    for step in ORDER:
        if step[0] == "mm":
            if multiplied == 0:
                load_weight.start()
                row_part[...] = jnp.zeros_like(row_part)
                row_x[col] = jnp.zeros((16, 128), jnp.float32)
            multiplied += 1
            final = multiplied == len(groups)
            matmul(groups[step[1]], first=multiplied == 1, last=final, width=512 if final else 1024)
        elif step[0][-1] == ">":
            if step[0] == "a>" and step[1] == (0, 0, 0):
                i = ("z+", "z-", "z2").index(step[2])
                turn(i + 1, a_src.at[i])
                push(a_src.at[i], at.at[own], a_sem.at[own], place[step[2]])
            else:
                send(step[0][:-1], step[1], step[2])
        else:
            ref, sem = piece(step[0][:-1], step[1])
            pltpu.make_async_copy(ref, ref, sem).wait()

    def spread(buf, slot, sem, sends, peer, slots, count):
        copies = []
        for i in range(1, count):
            copies.append(pltpu.make_async_remote_copy(
                src_ref=buf.at[slot], dst_ref=buf.at[slot], send_sem=sends.at[i], recv_sem=sem.at[slot],
                device_id=peer(i), device_id_type=MESH,
            ))
            copies[-1].start()

        def collect():
            for i in range(1, count):
                other = slots(i)
                pltpu.make_async_copy(buf.at[other], buf.at[other], sem.at[other]).wait()
            total = buf[0]
            for i in range(1, count):
                total = total + buf[i]
            return total

        sent.extend(copies)
        return collect

    col_collect = spread(col_x, group, col_sem, x_send, group_peer, group_slot, 16)
    for block in range(ROWS // 128):
        turned_part = row_part[pl.ds(block * 128, 128), :].T
        row_x[col, pl.ds(block, 1), :] = jnp.sum(turned_part, axis=0, keepdims=True)
    row_collect = spread(row_x, col, row_sem, y_send, col_peer, col_slot, 8)

    decay_rate = 1.0 - float(STEP) ** (-0.8)
    col_new = decay_rate * col_m[...] + (1.0 - decay_rate) * col_collect() / D
    col_out[...] = col_new
    col_scale[...] = lax.rsqrt(col_new)
    row_new = decay_rate * row_m[...] + (1.0 - decay_rate) * row_collect()[: ROWS // 128] / F
    row_out[...] = row_new
    row_scale = lax.rsqrt(row_new)
    for block in range(ROWS // 128):
        across = jnp.broadcast_to(row_scale[block:block + 1, :], (128, 128))
        row_col[pl.ds(block * 128, 128), :] = across.T

    def square_rows(block, total):
        r = pl.ds(pl.multiple_of(block * 64, 64), 64)
        line = jnp.zeros((64, 128), jnp.float32)
        for k in range(COLS // 128):
            s = pl.ds(k * 128, 128)
            value = g_ref[r, s] * col_scale[:, s]
            line = line + value * value
        factor = row_col[r, :]
        return total + line * factor * factor

    total = lax.fori_loop(0, ROWS // 64, square_rows, jnp.zeros((64, 128), jnp.float32))
    tot_a[group] = jnp.sum(total.reshape(8, 8, 128), axis=0)
    a_collect = spread(tot_a, group, ta_sem, ta_send, group_peer, group_slot, 16)
    tot_b[col] = a_collect()
    b_collect = spread(tot_b, col, tb_sem, tb_send, col_peer, col_slot, 8)
    for copy in sent:
        copy.wait_send()
    load_weight.wait()
    mean = jnp.sum(b_collect(), keepdims=True) / (D * F)
    clip_factor = jnp.maximum(1.0, jnp.sqrt(mean))
    col_scale[...] = col_scale[...] / clip_factor


def write_kernel(
    g_ref, w_ref, row_col, col_scale, row_new, col_new,
    new_weight, clipped, row_out, col_out, stage_w, stage_c, sem,
):
    relative = min(0.01, float(STEP) ** (-0.5))
    height, slots = 64, 6
    steps = ROWS // height

    def copies(i):
        r = pl.ds(i * height, height)
        s = i % slots
        return (
            pltpu.make_async_copy(stage_w.at[s], new_weight.at[r], sem.at[s, 0]),
            pltpu.make_async_copy(stage_c.at[s], clipped.at[r], sem.at[s, 1]),
        )

    for i in range(steps):
        if i >= slots:
            for copy in copies(i - slots):
                copy.wait()
        r = pl.ds(i * height, height)
        factor = row_col[r, :]
        for k in range(COLS // 128):
            s = pl.ds(k * 128, 128)
            value = g_ref[r, s] * factor * col_scale[:, s]
            stage_c[i % slots, :, s] = value.astype(jnp.bfloat16)
            stage_w[i % slots, :, s] = w_ref[r, s] - relative * value
        for copy in copies(i):
            copy.start()
    for block in range(ROWS // 128):
        row_out[pl.ds(block * 128, 128)] = row_new[block, :]
    for block in range(COLS // 128):
        col_out[pl.ds(block * 128, 128)] = col_new[0, block * 128:(block + 1) * 128]
    for i in range(steps - slots, steps):
        for copy in copies(i):
            copy.wait()


def body(activations, cotangent, weight, row_moment, col_moment):
    f32, bf16 = jnp.float32, jnp.bfloat16
    vmem, anywhere = pl.BlockSpec(memory_space=pltpu.VMEM), pl.BlockSpec(memory_space=pl.ANY)
    held = pl.pallas_call(
        gather_kernel,
        out_shape=(
            pltpu.VMEM((ROWS, COLS), f32),
            pltpu.VMEM((ROWS, COLS), f32),
            pltpu.VMEM((ROWS, 128), f32),
            pltpu.VMEM((1, COLS), f32),
            pltpu.VMEM((ROWS // 128, 128), f32),
            pltpu.VMEM((1, COLS), f32),
        ),
        in_specs=[anywhere, anywhere, anywhere, vmem, vmem],
        out_specs=(vmem,) * 6,
        scratch_shapes=[
            pltpu.VMEM((4, PIECE, ROWS), bf16),
            pltpu.VMEM((3, ROWS, PIECE), bf16),
            pltpu.VMEM((PIECES, ROWS, PIECE), bf16),
            pltpu.VMEM((PIECES, PIECE, COLS), bf16),
            pltpu.VMEM((ROWS, 128), f32),
            pltpu.VMEM((8, 16, 128), f32),
            pltpu.VMEM((16, 1, COLS), f32),
            pltpu.VMEM((16, 8, 128), f32),
            pltpu.VMEM((8, 8, 128), f32),
            pltpu.SemaphoreType.DMA((7,)),
            pltpu.SemaphoreType.DMA((SENDS,)),
            pltpu.SemaphoreType.DMA((PIECES + 2,)),
            pltpu.SemaphoreType.DMA((PIECES + 3,)),
            pltpu.SemaphoreType.DMA((16,)),
            pltpu.SemaphoreType.DMA((8,)),
            pltpu.SemaphoreType.DMA((16,)),
            pltpu.SemaphoreType.DMA((8,)),
            pltpu.SemaphoreType.DMA((8,)),
            pltpu.SemaphoreType.DMA((16,)),
            pltpu.SemaphoreType.DMA((16,)),
            pltpu.SemaphoreType.DMA((8,)),
        ],
        compiler_params=pltpu.CompilerParams(
            collective_id=0, has_side_effects=True, vmem_limit_bytes=38 << 20
        ),
    )(activations, cotangent, weight, row_moment.reshape(ROWS // 128, 128), col_moment.reshape(1, COLS))
    return pl.pallas_call(
        write_kernel,
        out_shape=(
            jax.ShapeDtypeStruct((ROWS, COLS), f32),
            jax.ShapeDtypeStruct((ROWS, COLS), bf16),
            jax.ShapeDtypeStruct((ROWS,), f32),
            jax.ShapeDtypeStruct((COLS,), f32),
        ),
        in_specs=[vmem] * 6,
        out_specs=(anywhere, anywhere, vmem, vmem),
        scratch_shapes=[
            pltpu.VMEM((6, 64, COLS), f32),
            pltpu.VMEM((6, 64, COLS), bf16),
            pltpu.SemaphoreType.DMA((6, 2)),
        ],
        compiler_params=pltpu.CompilerParams(vmem_limit_bytes=16 << 20),
    )(*held)


def solution(mesh):
    placed = (
        P(("dp", "col"), "row"),
        P(("dp", "row"), "col"),
        P(("row", "dp"), "col"),
        P(("row", "dp")),
        P("col"),
    )
    return jax.shard_map(
        body,
        mesh=mesh,
        in_specs=placed,
        out_specs=(P(("row", "dp"), "col"), P(("row", "dp"), "col"), P(("row", "dp")), P("col")),
        check_vma=False,
    )
```

time: 670 us -> 114 us (0.17)
  waiting for transfers between devices: 487 us -> 0 us
  Pallas kernels: 0 us -> 114 us
  blocking collectives: 114 us -> 0 us
  matrix products: 28 us -> 0 us
  other arithmetic: 26.6 us -> 0 us
  between operations: 14.5 us -> 0.64 us
    reduce_scatter x1 -> x0, waiting for transfers between devices: 315 us -> none  [body(): lax.psum_scatter(token_product(act_rows, cot_rows), 'dp', scatter_dimensi...]
    all_gather x2 -> x0, waiting for transfers between devices: 170 us -> none  [the longest x1 119 us: body(): act_rows = lax.all_gather(activations, 'col', axis=0, tiled=True)]
    psum x3 -> x0, blocking collectives: 114 us -> none  [the longest x1 62.2 us: body(): update_total = lax.psum(jnp.sum(update * update), ('dp', 'row', 'col'))]
    pallas_call x0 -> x2, Pallas kernels: none -> 114 us  [the longest x1 108 us: body(): pl.pallas_call(gather_kernel, out_shape=(pltpu.VMEM((ROWS, COLS), f32), p...]
    dot_general x1 -> x0, matrix products: 28 us -> none  [token_product(): lax.dot_general(left, right, (((0,), (0,)), ((), ())), preferred_element_...]
    convert_element_type x1 -> x0, other arithmetic: 13.6 us -> none  [body(): return (new_weight, clipped.astype(jnp.bfloat16), row_new, col_new)]
    reduce_sum x2 -> x0, other arithmetic: 11.7 us -> none  [the longest x1 7.04 us: body(): update_total = lax.psum(jnp.sum(update * update), ('dp', 'row', 'col'))]
  transfers between devices with their start and end apart: 3 -> 0, of which waited for: 3 -> 0; matrix products, arithmetic and copies ran while one was open for 0% -> 0% of each run, Pallas kernels for 0% -> 0%
where the time goes in v2:
time: 114 us
  Pallas kernels  114 us (100%)
    pallas_call x1, Pallas kernels, body(): pl.pallas_call(gather_kernel, out_shape=(pltpu.VMEM((ROWS, COLS), f32), p...  108 us
    pallas_call x1, Pallas kernels, body(): pl.pallas_call(write_kernel, out_shape=(jax.ShapeDtypeStruct((ROWS, COLS)...  5.8 us

profile of v2, /device:TPU:1, one launch (start us, length us, event | category | flops | bytes accessed | tf_op | source)
XLA Modules:
  0.0 114.2 jit_solution(14096122807426682402)
XLA Ops:
  0.6 107.8 %shard_map.84 = (f32[1152,2048]{1,0:T(8,128)S(1)}, f32[1152,2048]{1,0:T(8,128)S(1)}, f32[1152,128]{1,0:T(8,128)S(1)}, f32[1,2048]{1,0:T(1,128)S(1)}, f32[9,128]{1,0:T(8,128)S(1)}, /*index=5*/f32[1,2048]{1,0:T(1,128)S(1)}) custom-call(bf16[128,4608]{1,0:T(8,128)(2,1)} %act.1, bf16[256,2048]{1,0:T(8,128)(2,1)} %cot.1, f32[1152,2048]{1,0:T(8,128)} %weight.1, ...), custom_call_target="tpu_custom_call" | custom-call | tf_op jit(solution)/shard_map/pallas_call | solution.py:326
  108.4 5.8 %shard_map.85 = (f32[1152,2048]{1,0:T(8,128)}, bf16[1152,2048]{1,0:T(8,128)(2,1)}, f32[1152]{0:T(1024)}, f32[2048]{0:T(1024)}) custom-call(f32[1152,2048]{1,0:T(8,128)S(1)} %get-tuple-element.10.g_ref, f32[1152,2048]{1,0:T(8,128)S(1)} %get-tuple-element.11.w_ref, f32[1152,128]{1,0:T(8,128)S(1)} %get-tuple-element.12.row_col, ...), custom_call_target="tpu_custom_call" | custom-call | tf_op jit(solution)/shard_map/pallas_call | solution.py:365

commit v3 on v2

--- a/solution.py
+++ b/solution.py
@@ -25,37 +25,38 @@
 }
 PART_SEM = {"a0": 0, "a1": 1, "c0": 0, "c1": 1, "c2": 2}
 ORDER = (
-    ("c>", (0, 0, 0, 0), "z+"), ("a>", (0, 0, 0), "z-"), ("c>", (0, 0, 0, 0), "core"), ("c>", (0, 0, 0, 1), "core"),
-    ("c>", (0, 0, 0, 1), "z-"), ("c>", (0, 0, 0, 0), "x"), ("c<", (0, 0, 1, 0)), ("c<", (0, 0, 1, 1)),
-    ("a>", (0, 0, 0), "z+"), ("a<", (0, 0, -1)), ("a>", (0, 0, -1), "y+"), ("a<", (0, 0, 1)), ("a<", (1, 0, 0)),
-    ("a>", (1, 0, 0), "y-"), ("a<", (0, 1, 0)), ("a>", (0, 1, 0), "y+"), ("a>", (0, 1, 0), "y-"),
-    ("c<", (-1, 0, 0, 0)), ("c>", (-1, 0, 0, 0), "core"), ("c>", (-1, 0, 0, 0), "z+"), ("c>", (0, 0, 0, 0), "z-"),
-    ("a>", (1, 0, 0), "xh"), ("c<", (-1, 0, 1, 0)), ("a<", (0, 0, 2)), ("a>", (1, 0, 0), "y+"), ("a<", (1, 0, 1)),
-    ("a>", (1, 0, 1), "y-"), ("a<", (-1, 0, 0)), ("c<", (1, 0, 0, 1)), ("c>", (1, 0, 0, 1), "core"),
-    ("a>", (-1, 0, 0), "xh"), ("c<", (0, 1, 0, 0)), ("c>", (0, 1, 0, 0), "core"), ("c<", (1, 0, 1, 1)),
-    ("a<", (0, 1, -1)), ("a>", (-1, 0, 0), "y+"), ("a<", (0, 1, 1)), ("a>", (0, 1, 1), "y-"), ("c<", (0, 1, 1, 0)),
-    ("a>", (0, 0, 0), "z2"), ("a<", (1, 1, 0)), ("c>", (0, 0, 0, 1), "x"), ("a<", (1, 0, -1)),
-    ("a>", (1, 1, 0), "y+"), ("a<", (1, 0, 2)), ("a>", (1, 1, 0), "y-"), ("c<", (2, 0, 0, 0)),
-    ("c>", (2, 0, 0, 0), "core"), ("c>", (0, 0, 0, 1), "z+"), ("c>", (1, 0, 0, 1), "z-"), ("c<", (1, 0, 0, 0)),
-    ("c>", (1, 0, 0, 0), "core"), ("a<", (-1, 1, 0)), ("c<", (2, 0, 1, 0)), ("c<", (1, 0, 1, 0)), ("a<", (-1, 0, -1)),
-    ("a>", (-1, 1, 0), "y+"), ("a<", (0, 1, 2)), ("a>", (-1, 0, 0), "y-"), ("mm", "zero_near"),
-    ("c2>", (2, 0, 0, 0), "x"), ("a<", (2, 0, 0)), ("a<", (1, 1, -1)), ("a>", (2, 0, 0), "y+"), ("a<", (1, 1, 1)),
-    ("a>", (2, 0, 0), "y-"), ("c>", (0, 1, 0, 0), "z+"), ("c>", (0, 1, 0, 0), "z-"), ("a>", (2, 0, 0), "xh"),
-    ("c<", (0, 1, 0, 1)), ("c>", (0, 1, 0, 1), "core"), ("c<", (0, 1, 1, 1)), ("mm", "zero_far"),
-    ("a0>", (-1, 0, -1), "y+"), ("a>", (-1, 1, 0), "y-"), ("a<", (-1, 1, -1)), ("a<", (-1, 0, 1)),
-    ("c<", (-1, 0, 0, 1)), ("c>", (-1, 0, 0, 1), "core"), ("c<", (2, 0, 0, 1)), ("c>", (2, 0, 0, 1), "core"),
-    ("a>", (1, 0, 2), "xh"), ("c2<", (2, 1, 0, 0)), ("a>", (-1, 1, -1), "y+"), ("c<", (-1, 0, 1, 1)),
-    ("c<", (2, 0, 1, 1)), ("c>", (0, 1, 0, 1), "z+"), ("c>", (0, 1, 0, 1), "z-"), ("a<", (2, 0, -1)),
-    ("a<", (2, 0, 1)), ("a1>", (-1, 0, 1), "y-"), ("a<", (2, 1, 0)), ("c>", (2, 0, 0, 1), "x"), ("a0<", (-1, 0, 2)),
-    ("a>", (2, 1, 0), "y+"), ("a>", (2, 1, 0), "y-"), ("c<", (-1, 1, 0, 0)), ("c>", (-1, 1, 0, 0), "core"),
-    ("c<", (1, 1, 0, 0)), ("c>", (1, 1, 0, 0), "core"), ("a<", (-1, 1, 1)), ("a<", (1, 1, 2)), ("mm", "plus_near"),
-    ("a>", (2, 0, -1), "y+"), ("c0>", (-1, 1, 0, 0), "z+"), ("c1>", (1, 1, 0, 0), "z-"), ("c<", (-1, 1, 1, 0)),
-    ("c<", (1, 1, 1, 0)), ("a<", (-1, 1, 2)), ("a1<", (-1, 0, 2)), ("mm", "minus_near"), ("mm", "far_0"),
-    ("a<", (2, 1, -1)), ("a<", (2, 1, 1)), ("a>", (2, 1, 1), "y-"), ("c<", (-1, 1, 0, 1)),
-    ("c>", (-1, 1, 0, 1), "core"), ("c<", (1, 1, 0, 1)), ("c>", (1, 1, 0, 1), "core"), ("mm", "two_near"),
-    ("c<", (2, 1, 0, 1)), ("c>", (2, 1, 0, 1), "core"), ("c<", (-1, 1, 1, 1)), ("c0<", (2, 1, 0, 0)),
-    ("c1<", (2, 1, 0, 0)), ("c>", (2, 1, 0, 0), "core"), ("c<", (1, 1, 1, 1)), ("mm", "far_1"), ("c<", (2, 1, 1, 1)),
-    ("a<", (2, 0, 2)), ("c<", (2, 1, 1, 0)), ("mm", "two_far"), ("a<", (2, 1, 2)), ("mm", "two_last"),
+    ("a>", (0, 0, 0), "z+"), ("a>", (0, 0, 0), "z-"), ("c>", (0, 0, 0, 0), "core"), ("c>", (0, 0, 0, 1), "core"),
+    ("c>", (0, 0, 0, 0), "z+"), ("c>", (0, 0, 0, 1), "z-"), ("c>", (0, 0, 0, 1), "x"), ("c<", (0, 0, 1, 0)),
+    ("c<", (0, 0, 1, 1)), ("a<", (0, 0, -1)), ("a0>", (0, 0, -1), "y+"), ("a<", (0, 0, 1)), ("a1>", (0, 0, 1), "y-"),
+    ("a<", (-1, 0, 0)), ("a>", (-1, 0, 0), "y+"), ("a>", (-1, 0, 0), "y-"), ("a<", (1, 0, 0)), ("a<", (0, 1, 0)),
+    ("a0<", (0, 0, 2)), ("a>", (0, 1, 0), "y+"), ("a1<", (0, 0, 2)), ("a>", (0, 1, 0), "y-"), ("a>", (0, 0, 0), "z2"),
+    ("a>", (1, 0, 0), "xh"), ("a<", (-1, 0, -1)), ("a>", (1, 0, 0), "y+"), ("a<", (-1, 0, 1)),
+    ("a>", (1, 0, 0), "y-"), ("c<", (-1, 0, 0, 0)), ("c>", (-1, 0, 0, 0), "core"), ("c>", (0, 0, 0, 1), "z+"),
+    ("c>", (0, 0, 0, 0), "z-"), ("a>", (-1, 0, 0), "xh"), ("c<", (1, 0, 0, 1)), ("c>", (1, 0, 0, 1), "core"),
+    ("c<", (0, 1, 0, 1)), ("c>", (0, 1, 0, 1), "core"), ("c<", (-1, 0, 1, 0)), ("c<", (1, 0, 1, 1)),
+    ("c<", (0, 1, 1, 1)), ("a<", (0, 1, -1)), ("a>", (-1, 0, -1), "y+"), ("a<", (0, 1, 1)), ("a>", (0, 1, 1), "y-"),
+    ("a<", (2, 0, 0)), ("a<", (1, 1, 0)), ("a>", (2, 0, 0), "xh"), ("c>", (-1, 0, 0, 0), "z+"),
+    ("c>", (0, 1, 0, 1), "z-"), ("a<", (1, 0, -1)), ("a>", (1, 1, 0), "y+"), ("a<", (1, 0, 1)),
+    ("a>", (1, 1, 0), "y-"), ("a<", (-1, 1, 0)), ("c>", (0, 0, 0, 0), "x"), ("c<", (-1, 0, 0, 1)),
+    ("c>", (-1, 0, 0, 1), "core"), ("c<", (1, 0, 0, 0)), ("c>", (1, 0, 0, 0), "core"), ("a<", (-1, 0, 2)),
+    ("a>", (-1, 1, 0), "y+"), ("a<", (0, 1, 2)), ("a>", (-1, 1, 0), "y-"), ("mm", "zero_near"), ("a<", (2, 1, 0)),
+    ("c<", (-1, 0, 1, 1)), ("c<", (1, 0, 1, 0)), ("c>", (0, 1, 0, 1), "z+"), ("c>", (1, 0, 0, 1), "z-"),
+    ("a>", (-1, 0, 2), "xh"), ("a<", (1, 1, -1)), ("a>", (1, 1, -1), "y+"), ("a<", (1, 1, 1)),
+    ("a>", (1, 0, 1), "y-"), ("mm", "plus_near"), ("c<", (2, 0, 0, 0)), ("c>", (2, 0, 0, 0), "core"),
+    ("c<", (1, 1, 0, 1)), ("c>", (1, 1, 0, 1), "core"), ("c<", (0, 1, 0, 0)), ("c>", (0, 1, 0, 0), "core"),
+    ("c>", (2, 0, 0, 0), "x"), ("a<", (-1, 1, -1)), ("a>", (2, 0, 0), "y+"), ("c<", (2, 0, 1, 0)),
+    ("a>", (2, 1, 0), "y-"), ("a<", (-1, 1, 1)), ("mm", "minus_near"), ("c<", (1, 1, 1, 1)), ("c<", (0, 1, 1, 0)),
+    ("mm", "zero_far"), ("c>", (0, 1, 0, 0), "z+"), ("c>", (0, 1, 0, 0), "z-"), ("a<", (-1, 1, 2)), ("a<", (1, 1, 2)),
+    ("a>", (2, 1, 0), "y+"), ("a<", (1, 0, 2)), ("a>", (2, 0, 0), "y-"), ("mm", "near_last"), ("c<", (-1, 1, 0, 1)),
+    ("c>", (-1, 1, 0, 1), "core"), ("c<", (2, 0, 0, 1)), ("c>", (2, 0, 0, 1), "core"), ("mm", "far_1_0"),
+    ("c2>", (2, 0, 0, 1), "x"), ("c<", (-1, 1, 1, 1)), ("mm", "far_1_1"), ("c<", (2, 0, 1, 1)), ("a<", (2, 0, -1)),
+    ("a>", (2, 0, -1), "y+"), ("a<", (2, 1, 1)), ("a>", (2, 1, 1), "y-"), ("c0>", (-1, 1, 0, 1), "z+"),
+    ("c1>", (1, 1, 0, 1), "z-"), ("c<", (2, 1, 0, 0)), ("c>", (2, 1, 0, 0), "core"), ("a<", (2, 1, -1)),
+    ("a<", (2, 0, 1)), ("mm", "two_near"), ("c<", (2, 1, 1, 0)), ("c<", (-1, 1, 0, 0)), ("c>", (-1, 1, 0, 0), "core"),
+    ("c<", (1, 1, 0, 0)), ("c>", (1, 1, 0, 0), "core"), ("mm", "far_0_0"), ("c2<", (2, 1, 0, 1)),
+    ("c0<", (2, 1, 0, 1)), ("c1<", (2, 1, 0, 1)), ("c>", (2, 1, 0, 1), "core"), ("mm", "two_side"),
+    ("c<", (-1, 1, 1, 0)), ("c<", (1, 1, 1, 0)), ("mm", "far_0_1"), ("a<", (2, 0, 2)), ("a<", (2, 1, 2)),
+    ("c<", (2, 1, 1, 1)), ("mm", "two_last"),
 )
 
 
@@ -76,8 +77,10 @@
     def a_id(zo, xo, yo):
         return z_at[zo] * 8 + x_hi_at[xo] * 4 + y_at[yo]
 
+    half_at = (lax.rem(y + 1, 2), lax.rem(y, 2))
+
     def c_id(zo, xo, co, half):
-        return z_at[zo] * 8 + x_lo_at[xo] * 4 + core_at[co] * 2 + half
+        return z_at[zo] * 8 + x_lo_at[xo] * 4 + core_at[co] * 2 + half_at[half]
 
     place = {
         "z+": {"dp": z_at[1], "row": row, "col": col},
@@ -102,17 +105,31 @@
     def col_slot(i):
         return lax.rem(col + i, 8)
 
+    def plane_peer(i):
+        return {
+            "dp": lax.rem(z + i // 8, 4), "row": lax.rem(row + i // 2 % 4, 4), "col": lax.rem(x_hi + i % 2, 2) * 4 + y,
+        }
+
+    def plane_slot(i):
+        return (lax.rem(z + i // 8, 4) * 4 + lax.rem(row + i // 2 % 4, 4)) * 2 + lax.rem(x_hi + i % 2, 2)
+
+    def y_peer(i):
+        return {"dp": z, "row": row, "col": x_hi * 4 + lax.rem(y + i, 4)}
+
+    def y_slot(i):
+        return lax.rem(y + i, 4)
+
     offsets = (0, 1, -1, 2)
     load_act = []
     for i, o in enumerate(offsets):
         start = pl.multiple_of(z_at[o] * ROWS, 128)
         load_act.append(pltpu.make_async_copy(act.at[:, pl.ds(start, ROWS)], a_in.at[i], load_sem.at[i]))
         load_act[i].start()
-    mine = [c_id(0, 0, 0, half) for half in range(2)]
+    mine_at = z * 8 + x_lo * 4 + core * 2
     load_cot = []
     for half in range(2):
         load_cot.append(pltpu.make_async_copy(
-            cot.at[pl.ds(half * PIECE, PIECE)], ct.at[mine[half]], load_sem.at[4 + half]
+            cot.at[pl.ds(half * PIECE, PIECE)], ct.at[mine_at + half], load_sem.at[4 + half]
         ))
         load_cot[half].start()
 
@@ -182,23 +199,29 @@
     def cot_group(zo, xo):
         return [c_id(zo, xo, co, half) for co in range(2) for half in range(2)]
 
-    def far(half):
-        return [c_id(zo, 1, co, half) for zo in (-1, 1) for co in range(2)]
-
-    def early(half):
-        return [z_at[2] * 8 + half * 4 + y_at[yo] for yo in (0, 1, -1)]
+    def far(half, *planes):
+        return [c_id(zo, 1, co, half) for zo in (-1, 1) for co in planes]
+
+    def meet(zo, xo, *steps):
+        return [z_at[zo] * 8 + x_lo_at[xo] * 4 + y_at[yo] for yo in steps]
 
     groups = {
         "zero_near": cot_group(0, 0),
         "zero_far": cot_group(0, 1),
-        "plus_near": cot_group(1, 0),
-        "minus_near": cot_group(-1, 0),
-        "far_0": far(0),
-        "far_1": far(1),
-        "two_near": early(x_lo),
-        "two_far": early(1 - x_lo),
-        "two_last": [a_id(2, xo, 2) for xo in range(2)],
+        "plus_near": meet(1, 0, 0, 1, -1),
+        "minus_near": meet(-1, 0, 0, 1, -1),
+        "near_last": meet(1, 0, 2) + meet(-1, 0, 2),
+        "far_0": far(0, 0, 1),
+        "far_1": far(1, 0, 1),
+        "far_0_0": far(0, 0),
+        "far_0_1": far(0, 1),
+        "far_1_0": far(1, 0),
+        "far_1_1": far(1, 1),
+        "two_near": meet(2, 0, 0, 1, -1),
+        "two_side": meet(2, 1, 1, -1),
+        "two_last": meet(2, 1, 0, 2) + meet(2, 0, 2),
     }
+    rounds = len([step for step in ORDER if step[0] == "mm"])
 
     multiplied = 0
     for step in ORDER:
@@ -206,9 +229,8 @@
             if multiplied == 0:
                 load_weight.start()
                 row_part[...] = jnp.zeros_like(row_part)
-                row_x[col] = jnp.zeros((16, 128), jnp.float32)
             multiplied += 1
-            final = multiplied == len(groups)
+            final = multiplied == rounds
             matmul(groups[step[1]], first=multiplied == 1, last=final, width=512 if final else 1024)
         elif step[0][-1] == ">":
             if step[0] == "a>" and step[1] == (0, 0, 0):
@@ -252,7 +274,7 @@
     col_new = decay_rate * col_m[...] + (1.0 - decay_rate) * col_collect() / D
     col_out[...] = col_new
     col_scale[...] = lax.rsqrt(col_new)
-    row_new = decay_rate * row_m[...] + (1.0 - decay_rate) * row_collect()[: ROWS // 128] / F
+    row_new = decay_rate * row_m[...] + (1.0 - decay_rate) * row_collect() / F
     row_out[...] = row_new
     row_scale = lax.rsqrt(row_new)
     for block in range(ROWS // 128):
@@ -270,10 +292,11 @@
         return total + line * factor * factor
 
     total = lax.fori_loop(0, ROWS // 64, square_rows, jnp.zeros((64, 128), jnp.float32))
-    tot_a[group] = jnp.sum(total.reshape(8, 8, 128), axis=0)
-    a_collect = spread(tot_a, group, ta_sem, ta_send, group_peer, group_slot, 16)
-    tot_b[col] = a_collect()
-    b_collect = spread(tot_b, col, tb_sem, tb_send, col_peer, col_slot, 8)
+    plane = group * 2 + x_hi
+    tot_a[plane] = jnp.sum(total, axis=0, keepdims=True)
+    a_collect = spread(tot_a, plane, ta_sem, ta_send, plane_peer, plane_slot, 32)
+    tot_b[y] = a_collect()
+    b_collect = spread(tot_b, y, tb_sem, tb_send, y_peer, y_slot, 4)
     for copy in sent:
         copy.wait_send()
     load_weight.wait()
@@ -341,22 +364,22 @@
             pltpu.VMEM((PIECES, ROWS, PIECE), bf16),
             pltpu.VMEM((PIECES, PIECE, COLS), bf16),
             pltpu.VMEM((ROWS, 128), f32),
-            pltpu.VMEM((8, 16, 128), f32),
+            pltpu.VMEM((8, ROWS // 128, 128), f32),
             pltpu.VMEM((16, 1, COLS), f32),
-            pltpu.VMEM((16, 8, 128), f32),
-            pltpu.VMEM((8, 8, 128), f32),
+            pltpu.VMEM((32, 1, 128), f32),
+            pltpu.VMEM((4, 1, 128), f32),
             pltpu.SemaphoreType.DMA((7,)),
             pltpu.SemaphoreType.DMA((SENDS,)),
             pltpu.SemaphoreType.DMA((PIECES + 2,)),
             pltpu.SemaphoreType.DMA((PIECES + 3,)),
             pltpu.SemaphoreType.DMA((16,)),
             pltpu.SemaphoreType.DMA((8,)),
-            pltpu.SemaphoreType.DMA((16,)),
-            pltpu.SemaphoreType.DMA((8,)),
+            pltpu.SemaphoreType.DMA((32,)),
+            pltpu.SemaphoreType.DMA((4,)),
             pltpu.SemaphoreType.DMA((8,)),
             pltpu.SemaphoreType.DMA((16,)),
-            pltpu.SemaphoreType.DMA((16,)),
-            pltpu.SemaphoreType.DMA((8,)),
+            pltpu.SemaphoreType.DMA((32,)),
+            pltpu.SemaphoreType.DMA((4,)),
         ],
         compiler_params=pltpu.CompilerParams(
             collective_id=0, has_side_effects=True, vmem_limit_bytes=38 << 20

time: 114 us -> 114 us (level)
  Pallas kernels: 114 us -> 112 us
where the time goes in v3:
time: 114 us; the launch traced here: 113 us
  Pallas kernels  112 us (98%)
    pallas_call x1, Pallas kernels, body(): pl.pallas_call(gather_kernel, out_shape=(pltpu.VMEM((ROWS, COLS), f32), p...  107 us
    pallas_call x1, Pallas kernels, body(): pl.pallas_call(write_kernel, out_shape=(jax.ShapeDtypeStruct((ROWS, COLS)...  5.8 us

profile of v3, /device:TPU:1, one launch (start us, length us, event | category | flops | bytes accessed | tf_op | source)
XLA Modules:
  0.0 113.3 jit_solution(1592951234148193849)
XLA Ops:
  0.6 106.7 %shard_map.84 = (f32[1152,2048]{1,0:T(8,128)S(1)}, f32[1152,2048]{1,0:T(8,128)S(1)}, f32[1152,128]{1,0:T(8,128)S(1)}, f32[1,2048]{1,0:T(1,128)S(1)}, f32[9,128]{1,0:T(8,128)S(1)}, /*index=5*/f32[1,2048]{1,0:T(1,128)S(1)}) custom-call(bf16[128,4608]{1,0:T(8,128)(2,1)} %act.1, bf16[256,2048]{1,0:T(8,128)(2,1)} %cot.1, f32[1152,2048]{1,0:T(8,128)} %weight.1, ...), custom_call_target="tpu_custom_call" | custom-call | tf_op jit(solution)/shard_map/pallas_call | solution.py:349
  107.3 5.8 %shard_map.85 = (f32[1152,2048]{1,0:T(8,128)}, bf16[1152,2048]{1,0:T(8,128)(2,1)}, f32[1152]{0:T(1024)}, f32[2048]{0:T(1024)}) custom-call(f32[1152,2048]{1,0:T(8,128)S(1)} %get-tuple-element.10.g_ref, f32[1152,2048]{1,0:T(8,128)S(1)} %get-tuple-element.11.w_ref, f32[1152,128]{1,0:T(8,128)S(1)} %get-tuple-element.12.row_col, ...), custom_call_target="tpu_custom_call" | custom-call | tf_op jit(solution)/shard_map/pallas_call | solution.py:388

commit v4 on v3

--- a/solution.py
+++ b/solution.py
@@ -119,6 +119,10 @@
     def y_slot(i):
         return lax.rem(y + i, 4)
 
+    barrier = pltpu.get_barrier_semaphore()
+    for where in place.values():
+        pl.semaphore_signal(barrier, inc=1, device_id=where, device_id_type=MESH)
+
     offsets = (0, 1, -1, 2)
     load_act = []
     for i, o in enumerate(offsets):
@@ -132,10 +136,6 @@
             cot.at[pl.ds(half * PIECE, PIECE)], ct.at[mine_at + half], load_sem.at[4 + half]
         ))
         load_cot[half].start()
-
-    barrier = pltpu.get_barrier_semaphore()
-    for where in place.values():
-        pl.semaphore_signal(barrier, inc=1, device_id=where, device_id_type=MESH)
 
     sent = []
 
@@ -231,7 +231,7 @@
                 row_part[...] = jnp.zeros_like(row_part)
             multiplied += 1
             final = multiplied == rounds
-            matmul(groups[step[1]], first=multiplied == 1, last=final, width=512 if final else 1024)
+            matmul(groups[step[1]], first=multiplied == 1, last=final, width=1024)
         elif step[0][-1] == ">":
             if step[0] == "a>" and step[1] == (0, 0, 0):
                 i = ("z+", "z-", "z2").index(step[2])
@@ -245,7 +245,7 @@
 
     def spread(buf, slot, sem, sends, peer, slots, count):
         copies = []
-        for i in range(1, count):
+        for i in sorted(range(1, count), key=lambda i: abs(i // (count // 4) - 2)):
             copies.append(pltpu.make_async_remote_copy(
                 src_ref=buf.at[slot], dst_ref=buf.at[slot], send_sem=sends.at[i], recv_sem=sem.at[slot],
                 device_id=peer(i), device_id_type=MESH,
@@ -282,8 +282,8 @@
         row_col[pl.ds(block * 128, 128), :] = across.T
 
     def square_rows(block, total):
-        r = pl.ds(pl.multiple_of(block * 64, 64), 64)
-        line = jnp.zeros((64, 128), jnp.float32)
+        r = pl.ds(pl.multiple_of(block * 128, 128), 128)
+        line = jnp.zeros((128, 128), jnp.float32)
         for k in range(COLS // 128):
             s = pl.ds(k * 128, 128)
             value = g_ref[r, s] * col_scale[:, s]
@@ -291,7 +291,7 @@
         factor = row_col[r, :]
         return total + line * factor * factor
 
-    total = lax.fori_loop(0, ROWS // 64, square_rows, jnp.zeros((64, 128), jnp.float32))
+    total = lax.fori_loop(0, ROWS // 128, square_rows, jnp.zeros((128, 128), jnp.float32))
     plane = group * 2 + x_hi
     tot_a[plane] = jnp.sum(total, axis=0, keepdims=True)
     a_collect = spread(tot_a, plane, ta_sem, ta_send, plane_peer, plane_slot, 32)

time: 114 us -> 113 us (level)
  no operation moved by 1% of the time
where the time goes in v4:
time: 113 us
  Pallas kernels  112 us (99%)
    pallas_call x1, Pallas kernels, body(): pl.pallas_call(gather_kernel, out_shape=(pltpu.VMEM((ROWS, COLS), f32), p...  106 us
    pallas_call x1, Pallas kernels, body(): pl.pallas_call(write_kernel, out_shape=(jax.ShapeDtypeStruct((ROWS, COLS)...  5.8 us

profile of v4, /device:TPU:1, one launch (start us, length us, event | category | flops | bytes accessed | tf_op | source)
XLA Modules:
  0.0 112.9 jit_solution(5104844633803269992)
XLA Ops:
  0.6 106.3 %shard_map.84 = (f32[1152,2048]{1,0:T(8,128)S(1)}, f32[1152,2048]{1,0:T(8,128)S(1)}, f32[1152,128]{1,0:T(8,128)S(1)}, f32[1,2048]{1,0:T(1,128)S(1)}, f32[9,128]{1,0:T(8,128)S(1)}, /*index=5*/f32[1,2048]{1,0:T(1,128)S(1)}) custom-call(bf16[128,4608]{1,0:T(8,128)(2,1)} %act.1, bf16[256,2048]{1,0:T(8,128)(2,1)} %cot.1, f32[1152,2048]{1,0:T(8,128)} %weight.1, ...), custom_call_target="tpu_custom_call" | custom-call | tf_op jit(solution)/shard_map/pallas_call | solution.py:349
  107.0 5.8 %shard_map.85 = (f32[1152,2048]{1,0:T(8,128)}, bf16[1152,2048]{1,0:T(8,128)(2,1)}, f32[1152]{0:T(1024)}, f32[2048]{0:T(1024)}) custom-call(f32[1152,2048]{1,0:T(8,128)S(1)} %get-tuple-element.10.g_ref, f32[1152,2048]{1,0:T(8,128)S(1)} %get-tuple-element.11.w_ref, f32[1152,128]{1,0:T(8,128)S(1)} %get-tuple-element.12.row_col, ...), custom_call_target="tpu_custom_call" | custom-call | tf_op jit(solution)/shard_map/pallas_call | solution.py:388
